TPU v7x, 512 devices: a whole 4x4x16 slice. The times are simulated.
512 devices in a mesh: gx: 8 (over x, z_hi), gy: 4 (over y), gz: 16 (over z_lo, core).
Axes of the slice: x: 4, y: 4, z: 16 (z_hi: 2, z_lo: 8; z = z_hi * 8 + z_lo), core: 2. Of those that a mesh axis runs over, the one named last changes fastest.
Arguments:
- volume: float32 [128, 128, 1024], P('gz', 'gx', 'gy'), may hold values from -10 to 10
Outputs:
- diffused: float32 [128, 128, 1024], P('gz', 'gx', 'gy')
All inputs are finite; a program needn't handle non-finite values.
Results may differ from a plain program's by a relative error of at most 0.0003.
Values sent between devices are 32-bit elements; how exact they have to be, the bound alone decides.
A program may use at most 64 MiB of HBM per device.

v0:
```python
import jax
import jax.numpy as jnp
from jax import lax
from jax.sharding import PartitionSpec as P

kernel_taps = (0.41111229, 0.8007374, 1.0, 0.8007374, 0.41111229)
time_step = 3000.0
contrast = 0.1


def extended(shard, sides, width):
    for axis, dim in sides:
        peers, length = (lax.axis_size(axis), shard.shape[dim])
        up = [(i, (i + 1) % peers) for i in range(peers - 1)]
        down = [(j, i) for i, j in up]
        last = lax.slice_in_dim(shard, length - width, length, axis=dim)
        leading = lax.slice_in_dim(shard, 0, width, axis=dim)
        before = lax.ppermute(last, axis, up)
        after = lax.ppermute(leading, axis, down)
        shard = jnp.concatenate([before, shard, after], axis=dim)
    return shard


def blur_valid(values, first_dim):
    weight_sum = sum(kernel_taps)
    for axis_dim in range(first_dim, first_dim + 3):
        out_size = values.shape[axis_dim] - 4
        blurred = kernel_taps[0] / weight_sum * lax.slice_in_dim(values, 0, out_size, axis=axis_dim)
        for offset in range(1, 5):
            blurred = blurred + kernel_taps[offset] / weight_sum * lax.slice_in_dim(
                values, offset, offset + out_size, axis=axis_dim
            )
        values = blurred
    return values


def gradients(values, first_dim):
    result = []
    for axis_dim in range(first_dim, first_dim + 3):
        cropped = values
        for other_dim in range(first_dim, first_dim + 3):
            if other_dim != axis_dim:
                cropped = lax.slice_in_dim(cropped, 1, cropped.shape[other_dim] - 1, axis=other_dim)
        length = cropped.shape[axis_dim] - 2
        forward = lax.slice_in_dim(cropped, 2, length + 2, axis=axis_dim)
        behind = lax.slice_in_dim(cropped, 0, length, axis=axis_dim)
        result.append((forward - behind) * 0.5)
    return result


def shifted(values, stride, axis_dim, fill_value):
    length = values.shape[axis_dim]
    if abs(stride) >= length:
        return jnp.full(values.shape, fill_value, values.dtype)
    pad_shape = list(values.shape)
    pad_shape[axis_dim] = abs(stride)
    padding = jnp.full(tuple(pad_shape), fill_value, values.dtype)
    if stride > 0:
        return jnp.concatenate(
            [padding, lax.slice_in_dim(values, 0, length - stride, axis=axis_dim)], axis=axis_dim
        )
    return jnp.concatenate(
        [lax.slice_in_dim(values, -stride, length, axis=axis_dim), padding], axis=axis_dim
    )


def every_other(values, first_row, axis_dim):
    return lax.slice_in_dim(values, first_row, values.shape[axis_dim], stride=2, axis=axis_dim)


def reduce_solve(sub_diag, main_diag, super_diag, right_sides, axis_dim):
    length = main_diag.shape[axis_dim]
    if length == 1:
        return [right_side / main_diag for right_side in right_sides]
    even_sub = every_other(sub_diag, 0, axis_dim)
    odd_sub = every_other(sub_diag, 1, axis_dim)
    even_main = every_other(main_diag, 0, axis_dim)
    odd_main = every_other(main_diag, 1, axis_dim)
    even_super = every_other(super_diag, 0, axis_dim)
    odd_super = every_other(super_diag, 1, axis_dim)
    even_sides = [every_other(right_side, 0, axis_dim) for right_side in right_sides]
    odd_sides = [every_other(right_side, 1, axis_dim) for right_side in right_sides]
    lower_factor = -even_sub / shifted(odd_main, 1, axis_dim, 1.0)
    upper_factor = -even_super / odd_main
    reduced = reduce_solve(
        lower_factor * shifted(odd_sub, 1, axis_dim, 0.0),
        even_main + lower_factor * shifted(odd_super, 1, axis_dim, 0.0) + upper_factor * odd_sub,
        upper_factor * odd_super,
        [
            even_side + lower_factor * shifted(odd_side, 1, axis_dim, 0.0) + upper_factor * odd_side
            for even_side, odd_side in zip(even_sides, odd_sides)
        ],
        axis_dim,
    )
    result = []
    for even_part, odd_side in zip(reduced, odd_sides):
        odd_part = (
            odd_side - odd_sub * even_part - odd_super * shifted(even_part, -1, axis_dim, 0.0)
        ) / odd_main
        joined = jnp.stack([even_part, odd_part], axis=axis_dim + 1)
        joined_shape = list(even_part.shape)
        joined_shape[axis_dim] = 2 * joined_shape[axis_dim]
        result.append(joined.reshape(tuple(joined_shape)))
    return result


def face_pairs(diffusivity, axis_dim, position, device_count):
    cropped = diffusivity
    for other_dim in range(3):
        if other_dim != axis_dim:
            cropped = lax.slice_in_dim(cropped, 1, cropped.shape[other_dim] - 1, axis=other_dim)
    length = cropped.shape[axis_dim] - 2
    centre = lax.slice_in_dim(cropped, 1, length + 1, axis=axis_dim)
    following = lax.slice_in_dim(cropped, 2, length + 2, axis=axis_dim)
    before = lax.slice_in_dim(cropped, 0, length, axis=axis_dim)
    face_up = (centre + following) * 0.5
    face_down = (before + centre) * 0.5
    global_index = position * length + lax.broadcasted_iota(jnp.int32, face_up.shape, axis_dim)
    face_up = jnp.where(global_index < length * device_count - 1, face_up, 0.0)
    face_down = jnp.where(global_index > 0, face_down, 0.0)
    return (face_up, face_down)


def line_solve(values, face_up, axis_dim, stiffness):
    face_down = shifted(face_up, 1, axis_dim, 0.0)
    return reduce_solve(
        -stiffness * face_down,
        1.0 + stiffness * (face_down + face_up),
        -stiffness * face_up,
        [values],
        axis_dim,
    )[0]


def body(volume):
    stiffness = 3.0 * time_step
    positions = (lax.axis_index("gz"), lax.axis_index("gx"), lax.axis_index("gy"))
    counts = (lax.axis_size("gz"), lax.axis_size("gx"), lax.axis_size("gy"))
    widened = extended(volume, (("gx", 1), ("gy", 2), ("gz", 0)), 3)
    blurred = blur_valid(widened, 0)
    squares = jnp.stack([slope * slope for slope in gradients(blurred, 0)])
    square_halo = extended(squares, (("gx", 2), ("gy", 3), ("gz", 1)), 3)
    tensor = blur_valid(square_halo, 1)
    diffusivity = 1.0 / (1.0 + tensor / (contrast * contrast))
    up_z, down_z = face_pairs(diffusivity[0], 0, positions[0], counts[0])
    up_x, down_x = face_pairs(diffusivity[1], 1, positions[1], counts[1])
    up_y, down_y = face_pairs(diffusivity[2], 2, positions[2], counts[2])
    lines_x = (lambda pieces: line_solve(pieces[0], pieces[1], 1, stiffness))(
        (
            lax.all_to_all(volume, "gx", split_axis=0, concat_axis=1, tiled=True),
            lax.all_to_all(up_x, "gx", split_axis=0, concat_axis=1, tiled=True),
        )
    )
    solved_x = lax.all_to_all(lines_x, "gx", split_axis=1, concat_axis=0, tiled=True)
    lines_y = (lambda pieces: line_solve(pieces[0], pieces[1], 2, stiffness))(
        (
            lax.all_to_all(volume, "gy", split_axis=0, concat_axis=2, tiled=True),
            lax.all_to_all(up_y, "gy", split_axis=0, concat_axis=2, tiled=True),
        )
    )
    solved_y = lax.all_to_all(lines_y, "gy", split_axis=2, concat_axis=0, tiled=True)
    lines_z = (lambda pieces: line_solve(pieces[0], pieces[1], 0, stiffness))(
        (
            lax.all_to_all(volume, "gz", split_axis=1, concat_axis=0, tiled=True),
            lax.all_to_all(up_z, "gz", split_axis=1, concat_axis=0, tiled=True),
        )
    )
    solved_z = lax.all_to_all(lines_z, "gz", split_axis=0, concat_axis=1, tiled=True)
    summed = solved_x + solved_y + solved_z
    return summed / 3.0


def solution(mesh):
    return jax.shard_map(
        body,
        mesh=mesh,
        in_specs=(P("gz", "gx", "gy"),),
        out_specs=P("gz", "gx", "gy"),
        check_vma=False,
    )
```

profile of v0, /device:TPU:1, one launch (start us, length us, event | category | flops | bytes accessed | tf_op | source)
XLA Modules:
  0.0 376.5 jit_solution(18184623434700100287)
XLA Ops:
  0.0 1.6 copy.184
  2.4 16.3 %collective-permute-start = (f32[8,3,256]{2,0,1:T(8,128)S(1)}, f32[8,3,256]{2,0,1:T(8,128)S(1)}, u32[]{:S(2)}, u32[]{:S(2)}) collective-permute-start(f32[8,3,256]{2,0,1:T(8,128)S(1)} %get-tuple-element.90), channel_id=1, source_target_pairs={{0,64},{64,128},{128,192},{192,256},{256,320},{320,384},{384,448},... | collective-permute-start | bytes 73736 | tf_op jit(solution)/shard_map/ppermute | solution.py:18
  21.0 11.0 %collective-permute-done.1 = f32[8,3,256]{2,0,1:T(8,128)S(1)} collective-permute-done((f32[8,3,256]{2,0,1:T(8,128)S(1)}, f32[8,3,256]{2,0,1:T(8,128)S(1)}, u32[]{:S(2)}, u32[]{:S(2)}) %collective-permute-start.1) | collective-permute-done | bytes 24608 | tf_op jit(solution)/shard_map/ppermute | solution.py:19
  32.0 3.2 collective-permute-start.2
  36.8 3.7 collective-permute-done.3
  40.7 6.1 %collective-permute-start.4 = (f32[3,22,262]{2,0,1:T(4,128)S(1)}, f32[3,22,262]{2,0,1:T(4,128)S(1)}, u32[]{:S(2)}, u32[]{:S(2)}) collective-permute-start(f32[3,22,262]{2,0,1:T(4,128)S(1)} %get-tuple-element.62), channel_id=1, source_target_pairs={{0,1},{1,2},{2,3},{3,4},{4,5},{5,6},{6,7},{7,8},{8,9},{9,10},{10,1... | collective-permute-start | bytes 207512 | tf_op jit(solution)/shard_map/ppermute | solution.py:18
  46.8 1.9 collective-permute-start.5
  48.7 3.9 %all-to-all-start.3 = ((f32[8,16,256]{2,1,0:T(8,128)}), f32[8,16,256]{2,1,0:T(8,128)}, u32[]{:S(2)}, u32[]{:S(2)}) async-start(f32[8,16,256]{2,1,0:T(8,128)} %param.1), calls=%async_computation.3 | async-start | bytes 262144 | tf_op jit(solution)/shard_map/all_to_all | solution.py:157
  54.8 3.0 collective-permute-start.6
  59.3 16.2 %collective-permute-done.7 = f32[3,8,3,256]{3,1,2,0:T(8,128)S(1)} collective-permute-done((f32[3,8,3,256]{3,1,2,0:T(8,128)S(1)}, f32[3,8,3,256]{3,1,2,0:T(8,128)S(1)}, u32[]{:S(2)}, u32[]{:S(2)}) %collective-permute-start.7) | collective-permute-done | bytes 73760 | tf_op jit(solution)/shard_map/ppermute | solution.py:19
  75.7 3.7 collective-permute-start.8
  80.7 4.4 %collective-permute-done.8 = f32[3,8,22,3]{3,1,2,0:T(8,128)S(1)} collective-permute-done((f32[3,8,22,3]{3,1,2,0:T(8,128)S(1)}, f32[3,8,22,3]{3,1,2,0:T(8,128)S(1)}, u32[]{:S(2)}, u32[]{:S(2)}) %collective-permute-start.8) | collective-permute-done | bytes 6368 | tf_op jit(solution)/shard_map/ppermute | solution.py:18
  85.1 3.8 %collective-permute-done.9 = f32[3,8,22,3]{3,1,2,0:T(8,128)S(1)} collective-permute-done((f32[3,8,22,3]{3,1,2,0:T(8,128)S(1)}, f32[3,8,22,3]{3,1,2,0:T(8,128)S(1)}, u32[]{:S(2)}, u32[]{:S(2)}) %collective-permute-start.9) | collective-permute-done | bytes 6368 | tf_op jit(solution)/shard_map/ppermute | solution.py:19
  90.3 10.5 %collective-permute-start.10 = (f32[3,3,22,262]{3,1,2,0:T(4,128)}, f32[3,3,22,262]{3,1,2,0:T(4,128)S(1)}, u32[]{:S(2)}, u32[]{:S(2)}) collective-permute-start(f32[3,3,22,262]{3,1,2,0:T(4,128)} %get-tuple-element.47), channel_id=1, source_target_pairs={{0,1},{1,2},{2,3},{3,4},{4,5},{5,6},{6,7},{7,8},{8,9},{9,10},{10,1... | collective-permute-start | bytes 622520 | tf_op jit(solution)/shard_map/ppermute | solution.py:18
  100.8 1.9 collective-permute-start.11
  103.2 8.4 %all-to-all-start = ((f32[8,16,256]{2,1,0:T(8,128)}), f32[8,16,256]{2,1,0:T(8,128)}, u32[]{:S(2)}, u32[]{:S(2)}) async-start(f32[8,16,256]{2,1,0:T(8,128)} %param.1), calls=%async_computation | async-start | bytes 262144 | tf_op jit(solution)/shard_map/all_to_all | solution.py:150
  111.6 2.2 copy.188
  113.8 3.0 slice.1286
  116.8 4.1 %slice.1277 = f32[2,16,512]{1,2,0:T(8,128)} slice(f32[2,16,1024]{1,2,0:T(8,128)} %bitcast.240), slice={[0:2:1], [0:16:1], [0:1024:2]} | slice | bytes 131072 | tf_op jit(solution)/shard_map/slice | solution.py:68
  120.9 3.7 maximum_maximum_fusion
  124.6 2.3 fusion
  130.4 3.3 all-to-all-start.4
  135.7 2.8 all-to-all-done.4
  138.6 8.0 %all-to-all-start.6 = ((f32[8,16,256]{2,0,1:T(8,128)}), f32[8,16,256]{2,0,1:T(8,128)}, u32[]{:S(2)}, u32[]{:S(2)}) async-start(f32[8,16,256]{2,0,1:T(8,128)} %copy.184), calls=%async_computation.6 | async-start | bytes 262144 | tf_op jit(solution)/shard_map/all_to_all | solution.py:164
  146.9 1.6 pad_multiply_fusion
  148.5 3.0 slice.1290
  151.5 4.1 %slice.1283 = f32[2,16,512]{1,2,0:T(8,128)} slice(f32[2,16,1024]{1,2,0:T(8,128)} %get-tuple-element.44), slice={[0:2:1], [0:16:1], [0:1024:2]} | slice | bytes 131072 | tf_op jit(solution)/shard_map/slice | solution.py:68
  155.5 3.0 slice.1294
  158.5 4.1 %slice.1288 = f32[2,16,512]{1,2,0:T(8,128)} slice(f32[2,16,1024]{1,2,0:T(8,128)} %get-tuple-element.46), slice={[0:2:1], [0:16:1], [0:1024:2]} | slice | bytes 131072 | tf_op jit(solution)/shard_map/slice | solution.py:68
  163.4 2.2 slice.1293
  165.6 3.0 multiply_add_fusion.2
  172.7 1.7 slice.1300
  175.5 1.7 slice.1305
  177.2 2.2 multiply_add_fusion.4
  180.4 1.6 slice.1301
  183.0 1.6 slice.1304
  185.6 1.6 slice.1312
  187.2 1.6 slice.1308
  188.8 1.6 slice.1317
  190.4 2.1 multiply_add_fusion.7
  192.5 1.5 slice.1322
  194.0 1.5 slice.1313
  195.5 1.5 slice.1326
  197.1 1.5 slice.1316
  198.6 1.5 slice.1330
  200.1 1.5 slice.1324
  201.6 1.5 slice.1320
  203.2 1.5 slice.1329
  204.7 1.9 multiply_add_fusion.12
  218.2 1.6 multiply_add_fusion.18
  230.0 1.5 multiply_add_fusion.24
  242.0 1.5 multiply_add_fusion.30
  253.8 1.5 multiply_add_fusion.36
  276.0 14.1 %all-to-all-start.1 = ((f32[8,16,256]{2,1,0:T(8,128)}), f32[8,16,256]{2,1,0:T(8,128)S(1)}, u32[]{:S(2)}, u32[]{:S(2)}) async-start(f32[8,16,256]{2,1,0:T(8,128)} %copy.187), calls=%async_computation.1 | async-start | bytes 262144 | tf_op jit(solution)/shard_map/all_to_all | solution.py:151
  293.5 2.1 reshape.133
  297.4 7.1 %all-to-all-done.1 = f32[8,16,256]{2,1,0:T(8,128)S(1)} async-done(((f32[8,16,256]{2,1,0:T(8,128)}), f32[8,16,256]{2,1,0:T(8,128)S(1)}, u32[]{:S(2)}, u32[]{:S(2)}) %all-to-all-start.1) | async-done | bytes 131104 | tf_op jit(solution)/shard_map/all_to_all | solution.py:151
  304.5 13.9 %all-to-all-start.7 = ((f32[8,16,256]{2,0,1:T(8,128)}), f32[8,16,256]{2,0,1:T(8,128)S(1)}, u32[]{:S(2)}, u32[]{:S(2)}) async-start(f32[8,16,256]{2,0,1:T(8,128)} %fusion.30), calls=%async_computation.7 | async-start | bytes 262144 | tf_op jit(solution)/shard_map/all_to_all | solution.py:165
  322.2 8.2 %all-to-all-done.7 = f32[8,16,256]{2,0,1:T(8,128)S(1)} async-done(((f32[8,16,256]{2,0,1:T(8,128)}), f32[8,16,256]{2,0,1:T(8,128)S(1)}, u32[]{:S(2)}, u32[]{:S(2)}) %all-to-all-start.7) | async-done | bytes 131104 | tf_op jit(solution)/shard_map/all_to_all | solution.py:165
  330.4 3.5 all-to-all-start.5
  335.6 2.9 all-to-all-done.5
  338.5 3.4 all-to-all-start.2
  342.9 13.4 %all-to-all-done.2 = f32[1,128,256]{2,0,1:T(1,128)S(1)} async-done(((f32[1,128,256]{2,0,1:T(1,128)}), f32[1,128,256]{2,0,1:T(1,128)S(1)}, u32[]{:S(2)}, u32[]{:S(2)}) %all-to-all-start.2) | async-done | bytes 131104 | tf_op jit(solution)/shard_map/all_to_all | solution.py:154
  356.3 7.4 %all-to-all-start.8 = ((f32[128,1,256]{2,1,0:T(1,128)}), f32[128,1,256]{2,1,0:T(1,128)S(1)}, u32[]{:S(2)}, u32[]{:S(2)}) async-start(f32[128,1,256]{2,1,0:T(1,128)} %bitcast.99), calls=%async_computation.8 | async-start | bytes 262144 | tf_op jit(solution)/shard_map/all_to_all | solution.py:168
  367.1 8.6 %all-to-all-done.8 = f32[128,1,256]{2,1,0:T(1,128)S(1)} async-done(((f32[128,1,256]{2,1,0:T(1,128)}), f32[128,1,256]{2,1,0:T(1,128)S(1)}, u32[]{:S(2)}, u32[]{:S(2)}) %all-to-all-start.8) | async-done | bytes 131104 | tf_op jit(solution)/shard_map/all_to_all | solution.py:168
  (346 shorter events, 103.9 us)
Async XLA Ops:
  2.4 17.6 %collective-permute-start = (f32[8,3,256]{2,0,1:T(8,128)S(1)}, f32[8,3,256]{2,0,1:T(8,128)S(1)}, u32[]{:S(2)}, u32[]{:S(2)}) collective-permute-start(f32[8,3,256]{2,0,1:T(8,128)S(1)} %get-tuple-element.90), channel_id=1, source_target_pairs={{0,64},{64,128},{128,192},{192,256},{256,320},{320,384},{384,448},... | collective-permute-start | bytes 73736 | tf_op jit(solution)/shard_map/ppermute | solution.py:18
  18.7 13.3 %collective-permute-start.1 = (f32[8,3,256]{2,0,1:T(8,128)S(1)}, f32[8,3,256]{2,0,1:T(8,128)S(1)}, u32[]{:S(2)}, u32[]{:S(2)}) collective-permute-start(f32[8,3,256]{2,0,1:T(8,128)S(1)} %get-tuple-element.89), channel_id=1, source_target_pairs={{64,0},{128,64},{192,128},{256,192},{320,256},{384,320},{448,384},... | collective-permute-start | bytes 73736 | tf_op jit(solution)/shard_map/ppermute | solution.py:19
  32.0 4.8 %collective-permute-start.2 = (f32[8,22,3]{2,0,1:T(8,128)S(1)}, f32[8,22,3]{2,0,1:T(8,128)S(1)}, u32[]{:S(2)}, u32[]{:S(2)}) collective-permute-start(f32[8,22,3]{2,0,1:T(8,128)S(1)} %get-tuple-element.70), channel_id=1, source_target_pairs={{0,16},{16,32},{32,48},{1,17},{17,33},{33,49},{2,18},{18,34},{34,5... | collective-permute-start | bytes 6344 | tf_op jit(solution)/shard_map/ppermute | solution.py:18
  35.3 5.3 %collective-permute-start.3 = (f32[8,22,3]{2,0,1:T(8,128)S(1)}, f32[8,22,3]{2,0,1:T(8,128)S(1)}, u32[]{:S(2)}, u32[]{:S(2)}) collective-permute-start(f32[8,22,3]{2,0,1:T(8,128)S(1)} %get-tuple-element.71), channel_id=1, source_target_pairs={{16,0},{32,16},{48,32},{17,1},{33,17},{49,33},{18,2},{34,18},{50,3... | collective-permute-start | bytes 6344 | tf_op jit(solution)/shard_map/ppermute | solution.py:19
  40.7 12.0 %collective-permute-start.4 = (f32[3,22,262]{2,0,1:T(4,128)S(1)}, f32[3,22,262]{2,0,1:T(4,128)S(1)}, u32[]{:S(2)}, u32[]{:S(2)}) collective-permute-start(f32[3,22,262]{2,0,1:T(4,128)S(1)} %get-tuple-element.62), channel_id=1, source_target_pairs={{0,1},{1,2},{2,3},{3,4},{4,5},{5,6},{6,7},{7,8},{8,9},{9,10},{10,1... | collective-permute-start | bytes 207512 | tf_op jit(solution)/shard_map/ppermute | solution.py:18
  46.8 6.3 %collective-permute-start.5 = (f32[3,22,262]{2,0,1:T(4,128)S(1)}, f32[3,22,262]{2,0,1:T(4,128)S(1)}, u32[]{:S(2)}, u32[]{:S(2)}) collective-permute-start(f32[3,22,262]{2,0,1:T(4,128)S(1)} %get-tuple-element.63), channel_id=1, source_target_pairs={{1,0},{2,1},{3,2},{4,3},{5,4},{6,5},{7,6},{8,7},{9,8},{10,9},{11,1... | collective-permute-start | bytes 207512 | tf_op jit(solution)/shard_map/ppermute | solution.py:19
  48.7 54.4 %all-to-all-start.3 = ((f32[8,16,256]{2,1,0:T(8,128)}), f32[8,16,256]{2,1,0:T(8,128)}, u32[]{:S(2)}, u32[]{:S(2)}) async-start(f32[8,16,256]{2,1,0:T(8,128)} %param.1), calls=%async_computation.3 | async-start | bytes 262144 | tf_op jit(solution)/shard_map/all_to_all | solution.py:157
  54.8 4.4 %collective-permute-start.6 = (f32[3,8,3,256]{3,1,2,0:T(8,128)S(1)}, f32[3,8,3,256]{3,1,2,0:T(8,128)S(1)}, u32[]{:S(2)}, u32[]{:S(2)}) collective-permute-start(f32[3,8,3,256]{3,1,2,0:T(8,128)S(1)} %get-tuple-element.58), channel_id=1, source_target_pairs={{0,64},{64,128},{128,192},{192,256},{256,320},{320,384},{384,448},... | collective-permute-start | bytes 221192 | tf_op jit(solution)/shard_map/ppermute | solution.py:18
  57.9 17.6 %collective-permute-start.7 = (f32[3,8,3,256]{3,1,2,0:T(8,128)S(1)}, f32[3,8,3,256]{3,1,2,0:T(8,128)S(1)}, u32[]{:S(2)}, u32[]{:S(2)}) collective-permute-start(f32[3,8,3,256]{3,1,2,0:T(8,128)S(1)} %get-tuple-element.59), channel_id=1, source_target_pairs={{64,0},{128,64},{192,128},{256,192},{320,256},{384,320},{448,384},... | collective-permute-start | bytes 221192 | tf_op jit(solution)/shard_map/ppermute | solution.py:19
  59.3 30.0 %copy-start.3 = (f32[3,8,3,256]{3,1,2,0:T(8,128)}, f32[3,8,3,256]{3,1,2,0:T(8,128)S(1)}, u32[]{:S(2)}) copy-start(f32[3,8,3,256]{3,1,2,0:T(8,128)S(1)} %collective-permute-done.6) | copy-start | bytes 221188
  75.5 13.8 %copy-start.5 = (f32[3,8,3,256]{3,1,2,0:T(8,128)}, f32[3,8,3,256]{3,1,2,0:T(8,128)S(1)}, u32[]{:S(2)}) copy-start(f32[3,8,3,256]{3,1,2,0:T(8,128)S(1)} %collective-permute-done.7) | copy-start | bytes 221188
  75.7 9.4 %collective-permute-start.8 = (f32[3,8,22,3]{3,1,2,0:T(8,128)S(1)}, f32[3,8,22,3]{3,1,2,0:T(8,128)S(1)}, u32[]{:S(2)}, u32[]{:S(2)}) collective-permute-start(f32[3,8,22,3]{3,1,2,0:T(8,128)S(1)} %get-tuple-element.49), channel_id=1, source_target_pairs={{0,16},{16,32},{32,48},{1,17},{17,33},{33,49},{2,18},{18,34},{34,5... | collective-permute-start | bytes 19016 | tf_op jit(solution)/shard_map/ppermute | solution.py:18
  79.4 9.5 %collective-permute-start.9 = (f32[3,8,22,3]{3,1,2,0:T(8,128)S(1)}, f32[3,8,22,3]{3,1,2,0:T(8,128)S(1)}, u32[]{:S(2)}, u32[]{:S(2)}) collective-permute-start(f32[3,8,22,3]{3,1,2,0:T(8,128)S(1)} %get-tuple-element.50), channel_id=1, source_target_pairs={{16,0},{32,16},{48,32},{17,1},{33,17},{49,33},{18,2},{34,18},{50,3... | collective-permute-start | bytes 19016 | tf_op jit(solution)/shard_map/ppermute | solution.py:19
  90.3 30.6 %collective-permute-start.10 = (f32[3,3,22,262]{3,1,2,0:T(4,128)}, f32[3,3,22,262]{3,1,2,0:T(4,128)S(1)}, u32[]{:S(2)}, u32[]{:S(2)}) collective-permute-start(f32[3,3,22,262]{3,1,2,0:T(4,128)} %get-tuple-element.47), channel_id=1, source_target_pairs={{0,1},{1,2},{2,3},{3,4},{4,5},{5,6},{6,7},{7,8},{8,9},{9,10},{10,1... | collective-permute-start | bytes 622520 | tf_op jit(solution)/shard_map/ppermute | solution.py:18
  100.8 20.1 %collective-permute-start.11 = (f32[3,3,22,262]{3,1,2,0:T(4,128)}, f32[3,3,22,262]{3,1,2,0:T(4,128)}, u32[]{:S(2)}, u32[]{:S(2)}) collective-permute-start(f32[3,3,22,262]{3,1,2,0:T(4,128)} %get-tuple-element.48), channel_id=1, source_target_pairs={{1,0},{2,1},{3,2},{4,3},{5,4},{6,5},{7,6},{8,7},{9,8},{10,9},{11,1... | collective-permute-start | bytes 622520 | tf_op jit(solution)/shard_map/ppermute | solution.py:19
  103.2 27.3 %all-to-all-start = ((f32[8,16,256]{2,1,0:T(8,128)}), f32[8,16,256]{2,1,0:T(8,128)}, u32[]{:S(2)}, u32[]{:S(2)}) async-start(f32[8,16,256]{2,1,0:T(8,128)} %param.1), calls=%async_computation | async-start | bytes 262144 | tf_op jit(solution)/shard_map/all_to_all | solution.py:150
  120.9 3.7 copy-start.4
  120.9 3.7 copy-start.6
  130.4 8.1 %all-to-all-start.4 = ((f32[8,16,256]{2,1,0:T(8,128)}), f32[8,16,256]{2,1,0:T(8,128)S(1)}, u32[]{:S(2)}, u32[]{:S(2)}) async-start(f32[8,16,256]{2,1,0:T(8,128)} %copy.189), calls=%async_computation.4 | async-start | bytes 262144 | tf_op jit(solution)/shard_map/all_to_all | solution.py:158
  135.7 10.9 %copy-start.1 = (f32[1,128,256]{2,0,1:T(1,128)}, f32[1,128,256]{2,0,1:T(1,128)S(1)}, u32[]{:S(2)}) copy-start(f32[1,128,256]{2,0,1:T(1,128)S(1)} %all_to_all.106) | copy-start | bytes 393220
  135.7 11.2 %copy-start.7 = (f32[1,64,256]{2,0,1:T(1,128)}, f32[1,64,256]{2,0,1:T(1,128)S(1)}, u32[]{:S(2)}) copy-start(f32[1,64,256]{2,0,1:T(1,128)S(1)} %slice.1195) | copy-start | bytes 196612
  138.6 137.4 %all-to-all-start.6 = ((f32[8,16,256]{2,0,1:T(8,128)}), f32[8,16,256]{2,0,1:T(8,128)}, u32[]{:S(2)}, u32[]{:S(2)}) async-start(f32[8,16,256]{2,0,1:T(8,128)} %copy.184), calls=%async_computation.6 | async-start | bytes 262144 | tf_op jit(solution)/shard_map/all_to_all | solution.py:164
  265.5 9.4 %copy-start = (f32[2,16,128]{1,2,0:T(8,128)S(1)}, f32[2,16,128]{1,2,0:T(8,128)}, u32[]{:S(2)}) copy-start(f32[2,16,128]{1,2,0:T(8,128)} %slice.1308) | copy-start | bytes 49156
  276.0 28.5 %all-to-all-start.1 = ((f32[8,16,256]{2,1,0:T(8,128)}), f32[8,16,256]{2,1,0:T(8,128)S(1)}, u32[]{:S(2)}, u32[]{:S(2)}) async-start(f32[8,16,256]{2,1,0:T(8,128)} %copy.187), calls=%async_computation.1 | async-start | bytes 262144 | tf_op jit(solution)/shard_map/all_to_all | solution.py:151
  293.5 25.4 %copy-start.2 = (f32[1,128,256]{2,0,1:T(1,128)S(1)}, f32[1,128,256]{2,0,1:T(1,128)}, u32[]{:S(2)}) copy-start(f32[1,128,256]{2,0,1:T(1,128)} %copy-done.1) | copy-start | bytes 393220
  293.5 25.4 %slice-start = ((f32[1,64,256]{2,0,1:T(1,128)}), f32[1,63,256]{2,0,1:T(1,128)S(1)}, s32[]{:S(2)}) async-start(f32[1,64,256]{2,0,1:T(1,128)} %copy-done.7), calls=%async_computation.9 | async-start | bytes 129024 | tf_op jit(solution)/shard_map/slice | solution.py:60
  304.5 25.9 %all-to-all-start.7 = ((f32[8,16,256]{2,0,1:T(8,128)}), f32[8,16,256]{2,0,1:T(8,128)S(1)}, u32[]{:S(2)}, u32[]{:S(2)}) async-start(f32[8,16,256]{2,0,1:T(8,128)} %fusion.30), calls=%async_computation.7 | async-start | bytes 262144 | tf_op jit(solution)/shard_map/all_to_all | solution.py:165
  330.4 8.1 %all-to-all-start.5 = ((f32[4,1,8192]{2,1,0:T(1,128)}), f32[4,1,8192]{2,1,0:T(1,128)S(1)}, u32[]{:S(2)}, u32[]{:S(2)}) async-start(f32[4,1,8192]{2,1,0:T(1,128)} %reshape.133), calls=%async_computation.5 | async-start | bytes 262144 | tf_op jit(solution)/shard_map/all_to_all | solution.py:161
  338.5 17.8 %all-to-all-start.2 = ((f32[1,128,256]{2,0,1:T(1,128)}), f32[1,128,256]{2,0,1:T(1,128)S(1)}, u32[]{:S(2)}, u32[]{:S(2)}) async-start(f32[1,128,256]{2,0,1:T(1,128)} %bitcast.24), calls=%async_computation.2 | async-start | bytes 262144 | tf_op jit(solution)/shard_map/all_to_all | solution.py:154
  356.3 19.4 %all-to-all-start.8 = ((f32[128,1,256]{2,1,0:T(1,128)}), f32[128,1,256]{2,1,0:T(1,128)S(1)}, u32[]{:S(2)}, u32[]{:S(2)}) async-start(f32[128,1,256]{2,1,0:T(1,128)} %bitcast.99), calls=%async_computation.8 | async-start | bytes 262144 | tf_op jit(solution)/shard_map/all_to_all | solution.py:168
where the time goes:
time: 382 us; the launch traced here: 376 us
  local copies, waits for them, and re-layouts  132 us (35%)
  starting transfers between devices  118 us (31%)
  waiting for transfers between devices  82.8 us (22%)
  other arithmetic  41.6 us (11%)
    slice x133, local copies, waits for them, and re-layouts, every_other(): lax.slice_in_dim(values, first_row, values.shape[axis_dim], stride=2, axi...  112 us
    ppermute x6, starting transfers between devices, extended(): before = lax.ppermute(last, axis, up)  42.8 us
    ppermute x6, waiting for transfers between devices, extended(): after = lax.ppermute(leading, axis, down)  35.1 us
    add x21, other arithmetic, reduce_solve(): even_side + lower_factor * shifted(odd_side, 1, axis_dim, 0.0)  16.7 us
    all_to_all x1, starting transfers between devices, body(): lax.all_to_all(up_x, 'gx', split_axis=0, concat_axis=1, tiled=True)  14.1 us
    all_to_all x1, starting transfers between devices, body(): lax.all_to_all(up_z, 'gz', split_axis=1, concat_axis=0, tiled=True)  13.9 us
    all_to_all x1, waiting for transfers between devices, body(): lax.all_to_all(lines_x, 'gx', split_axis=1, concat_axis=0, tiled=True)  13.4 us
    ppermute x6, starting transfers between devices, extended(): after = lax.ppermute(leading, axis, down)  9.01 us
  transfers between devices with their start and end apart: 21, of which 14 were waited for; matrix products, arithmetic and copies ran while one was open for 45% of the time, Pallas kernels for 0%

commit v1 on v0

--- a/solution.py
+++ b/solution.py
@@ -158,7 +158,10 @@
             lax.all_to_all(up_y, "gy", split_axis=0, concat_axis=2, tiled=True),
         )
     )
-    solved_y = lax.all_to_all(lines_y, "gy", split_axis=2, concat_axis=0, tiled=True)
+    solved_y = jnp.concatenate(
+        lax.all_to_all(jnp.stack(jnp.split(lines_y, lax.axis_size("gy"), axis=2)), "gy", 0, 0),
+        axis=0,
+    )
     lines_z = (lambda pieces: line_solve(pieces[0], pieces[1], 0, stiffness))(
         (
             lax.all_to_all(volume, "gz", split_axis=1, concat_axis=0, tiled=True),

time: 382 us -> 377 us (0.987)
  local copies, waits for them, and re-layouts: 132 us -> 124 us
  waiting for transfers between devices: 82.8 us -> 88.6 us
  transfers between devices with their start and end apart: 21 -> 21, of which waited for: 14 -> 14; matrix products, arithmetic and copies ran while one was open for 45% -> 43% of each run, Pallas kernels for 0% -> 0%
where the time goes in v1:
time: 377 us; the launch traced here: 372 us
  local copies, waits for them, and re-layouts  124 us (33%)
  starting transfers between devices  117 us (31%)
  waiting for transfers between devices  88.6 us (24%)
  other arithmetic  40.8 us (11%)
    slice x133, local copies, waits for them, and re-layouts, every_other(): lax.slice_in_dim(values, first_row, values.shape[axis_dim], stride=2, axi...  109 us
    ppermute x6, starting transfers between devices, extended(): before = lax.ppermute(last, axis, up)  42.9 us
    ppermute x6, waiting for transfers between devices, extended(): after = lax.ppermute(leading, axis, down)  35.2 us
    add x21, other arithmetic, reduce_solve(): even_side + lower_factor * shifted(odd_side, 1, axis_dim, 0.0)  16.7 us
    all_to_all x1, starting transfers between devices, body(): lax.all_to_all(up_x, 'gx', split_axis=0, concat_axis=1, tiled=True)  14.1 us
    all_to_all x1, starting transfers between devices, body(): lax.all_to_all(up_z, 'gz', split_axis=1, concat_axis=0, tiled=True)  13.9 us
    all_to_all x1, waiting for transfers between devices, body(): lax.all_to_all(lines_x, 'gx', split_axis=1, concat_axis=0, tiled=True)  11.5 us
    all_to_all x1, waiting for transfers between devices, body(): lax.all_to_all(up_x, 'gx', split_axis=0, concat_axis=1, tiled=True)  10.7 us
  transfers between devices with their start and end apart: 21, of which 14 were waited for; matrix products, arithmetic and copies ran while one was open for 43% of the time, Pallas kernels for 0%

profile of v1, /device:TPU:1, one launch (start us, length us, event | category | flops | bytes accessed | tf_op | source)
XLA Modules:
  0.0 371.8 jit_solution(5322520439602190186)
XLA Ops:
  0.0 1.6 copy.184
  2.4 16.3 %collective-permute-start = (f32[8,3,256]{2,0,1:T(8,128)S(1)}, f32[8,3,256]{2,0,1:T(8,128)S(1)}, u32[]{:S(2)}, u32[]{:S(2)}) collective-permute-start(f32[8,3,256]{2,0,1:T(8,128)S(1)} %get-tuple-element.94), channel_id=1, source_target_pairs={{0,64},{64,128},{128,192},{192,256},{256,320},{320,384},{384,448},... | collective-permute-start | bytes 73736 | tf_op jit(solution)/shard_map/ppermute | solution.py:18
  21.0 11.0 %collective-permute-done.1 = f32[8,3,256]{2,0,1:T(8,128)S(1)} collective-permute-done((f32[8,3,256]{2,0,1:T(8,128)S(1)}, f32[8,3,256]{2,0,1:T(8,128)S(1)}, u32[]{:S(2)}, u32[]{:S(2)}) %collective-permute-start.1) | collective-permute-done | bytes 24608 | tf_op jit(solution)/shard_map/ppermute | solution.py:19
  32.0 3.2 collective-permute-start.2
  36.8 3.7 %collective-permute-done.3 = f32[8,22,3]{2,0,1:T(8,128)S(1)} collective-permute-done((f32[8,22,3]{2,0,1:T(8,128)S(1)}, f32[8,22,3]{2,0,1:T(8,128)S(1)}, u32[]{:S(2)}, u32[]{:S(2)}) %collective-permute-start.3) | collective-permute-done | bytes 2144 | tf_op jit(solution)/shard_map/ppermute | solution.py:19
  40.7 6.1 %collective-permute-start.4 = (f32[3,22,262]{2,0,1:T(4,128)S(1)}, f32[3,22,262]{2,0,1:T(4,128)S(1)}, u32[]{:S(2)}, u32[]{:S(2)}) collective-permute-start(f32[3,22,262]{2,0,1:T(4,128)S(1)} %get-tuple-element.66), channel_id=1, source_target_pairs={{0,1},{1,2},{2,3},{3,4},{4,5},{5,6},{6,7},{7,8},{8,9},{9,10},{10,1... | collective-permute-start | bytes 207512 | tf_op jit(solution)/shard_map/ppermute | solution.py:18
  46.8 1.9 collective-permute-start.5
  48.7 3.9 %all-to-all-start.3 = ((f32[8,16,256]{2,1,0:T(8,128)}), f32[8,16,256]{2,1,0:T(8,128)S(1)}, u32[]{:S(2)}, u32[]{:S(2)}) async-start(f32[8,16,256]{2,1,0:T(8,128)} %param.1), calls=%async_computation.3 | async-start | bytes 262144 | tf_op jit(solution)/shard_map/all_to_all | solution.py:157
  54.9 3.0 collective-permute-start.6
  59.3 16.2 %collective-permute-done.7 = f32[3,8,3,256]{3,1,2,0:T(8,128)S(1)} collective-permute-done((f32[3,8,3,256]{3,1,2,0:T(8,128)S(1)}, f32[3,8,3,256]{3,1,2,0:T(8,128)S(1)}, u32[]{:S(2)}, u32[]{:S(2)}) %collective-permute-start.7) | collective-permute-done | bytes 73760 | tf_op jit(solution)/shard_map/ppermute | solution.py:19
  75.7 3.7 %collective-permute-start.8 = (f32[3,8,22,3]{3,1,2,0:T(8,128)S(1)}, f32[3,8,22,3]{3,1,2,0:T(8,128)S(1)}, u32[]{:S(2)}, u32[]{:S(2)}) collective-permute-start(f32[3,8,22,3]{3,1,2,0:T(8,128)S(1)} %get-tuple-element.53), channel_id=1, source_target_pairs={{0,16},{16,32},{32,48},{1,17},{17,33},{33,49},{2,18},{18,34},{34,5... | collective-permute-start | bytes 19016 | tf_op jit(solution)/shard_map/ppermute | solution.py:18
  80.7 4.3 %collective-permute-done.8 = f32[3,8,22,3]{3,1,2,0:T(8,128)S(1)} collective-permute-done((f32[3,8,22,3]{3,1,2,0:T(8,128)S(1)}, f32[3,8,22,3]{3,1,2,0:T(8,128)S(1)}, u32[]{:S(2)}, u32[]{:S(2)}) %collective-permute-start.8) | collective-permute-done | bytes 6368 | tf_op jit(solution)/shard_map/ppermute | solution.py:18
  85.0 3.8 %collective-permute-done.9 = f32[3,8,22,3]{3,1,2,0:T(8,128)S(1)} collective-permute-done((f32[3,8,22,3]{3,1,2,0:T(8,128)S(1)}, f32[3,8,22,3]{3,1,2,0:T(8,128)S(1)}, u32[]{:S(2)}, u32[]{:S(2)}) %collective-permute-start.9) | collective-permute-done | bytes 6368 | tf_op jit(solution)/shard_map/ppermute | solution.py:19
  90.2 10.6 %collective-permute-start.10 = (f32[3,3,22,262]{3,1,2,0:T(4,128)}, f32[3,3,22,262]{3,1,2,0:T(4,128)}, u32[]{:S(2)}, u32[]{:S(2)}) collective-permute-start(f32[3,3,22,262]{3,1,2,0:T(4,128)} %get-tuple-element.51), channel_id=1, source_target_pairs={{0,1},{1,2},{2,3},{3,4},{4,5},{5,6},{6,7},{7,8},{8,9},{9,10},{10,1... | collective-permute-start | bytes 622520 | tf_op jit(solution)/shard_map/ppermute | solution.py:18
  100.8 1.9 collective-permute-start.11
  103.1 8.4 %all-to-all-start = ((f32[8,16,256]{2,1,0:T(8,128)}), f32[8,16,256]{2,1,0:T(8,128)S(1)}, u32[]{:S(2)}, u32[]{:S(2)}) async-start(f32[8,16,256]{2,1,0:T(8,128)} %param.1), calls=%async_computation | async-start | bytes 262144 | tf_op jit(solution)/shard_map/all_to_all | solution.py:150
  112.9 3.0 slice.1286
  115.9 4.1 %slice.1277 = f32[2,16,512]{1,2,0:T(8,128)} slice(f32[2,16,1024]{1,2,0:T(8,128)} %bitcast.242), slice={[0:2:1], [0:16:1], [0:1024:2]} | slice | bytes 131072 | tf_op jit(solution)/shard_map/slice | solution.py:68
  120.0 3.7 maximum_maximum_fusion
  123.7 2.4 fusion
  129.6 3.3 all-to-all-start.4
  134.0 3.7 %all-to-all-done.4 = f32[8,16,256]{2,1,0:T(8,128)S(1)} async-done(((f32[8,16,256]{2,1,0:T(8,128)}), f32[8,16,256]{2,1,0:T(8,128)S(1)}, u32[]{:S(2)}, u32[]{:S(2)}) %all-to-all-start.4) | async-done | bytes 131104 | tf_op jit(solution)/shard_map/all_to_all | solution.py:158
  137.8 8.0 %all-to-all-start.6 = ((f32[8,16,256]{2,0,1:T(8,128)}), f32[8,16,256]{2,0,1:T(8,128)}, u32[]{:S(2)}, u32[]{:S(2)}) async-start(f32[8,16,256]{2,0,1:T(8,128)} %copy.184), calls=%async_computation.6 | async-start | bytes 262144 | tf_op jit(solution)/shard_map/all_to_all | solution.py:167
  146.1 1.6 pad_multiply_fusion
  147.7 3.0 slice.1290
  150.7 4.1 %slice.1283 = f32[2,16,512]{1,2,0:T(8,128)} slice(f32[2,16,1024]{1,2,0:T(8,128)} %get-tuple-element.48), slice={[0:2:1], [0:16:1], [0:1024:2]} | slice | bytes 131072 | tf_op jit(solution)/shard_map/slice | solution.py:68
  154.8 3.0 slice.1294
  157.8 4.1 %slice.1288 = f32[2,16,512]{1,2,0:T(8,128)} slice(f32[2,16,1024]{1,2,0:T(8,128)} %get-tuple-element.50), slice={[0:2:1], [0:16:1], [0:1024:2]} | slice | bytes 131072 | tf_op jit(solution)/shard_map/slice | solution.py:68
  162.6 2.2 slice.1293
  164.8 3.0 multiply_add_fusion.2
  169.7 1.7 slice.1292
  173.4 1.7 slice.1305
  175.1 2.3 multiply_add_fusion.4
  179.1 1.6 slice.1304
  181.7 1.6 slice.1312
  183.3 1.6 slice.1308
  184.9 1.6 slice.1317
  186.5 2.1 multiply_add_fusion.7
  188.6 1.5 slice.1322
  190.1 1.5 slice.1313
  191.7 1.5 slice.1326
  193.2 1.5 slice.1316
  194.7 1.5 slice.1330
  196.3 1.5 slice.1324
  197.8 1.5 slice.1320
  199.3 1.5 slice.1329
  200.9 1.9 multiply_add_fusion.12
  208.6 1.5 slice.1342
  210.0 1.5 slice.1336
  211.5 1.5 slice.1332
  212.9 1.5 slice.1341
  214.4 1.7 multiply_add_fusion.18
  226.4 1.5 multiply_add_fusion.24
  238.4 1.5 multiply_add_fusion.30
  272.2 14.1 %all-to-all-start.1 = ((f32[8,16,256]{2,1,0:T(8,128)}), f32[8,16,256]{2,1,0:T(8,128)S(1)}, u32[]{:S(2)}, u32[]{:S(2)}) async-start(f32[8,16,256]{2,1,0:T(8,128)} %copy.187), calls=%async_computation.1 | async-start | bytes 262144 | tf_op jit(solution)/shard_map/all_to_all | solution.py:151
  290.0 10.7 %all-to-all-done.1 = f32[8,16,256]{2,1,0:T(8,128)S(1)} async-done(((f32[8,16,256]{2,1,0:T(8,128)}), f32[8,16,256]{2,1,0:T(8,128)S(1)}, u32[]{:S(2)}, u32[]{:S(2)}) %all-to-all-start.1) | async-done | bytes 131104 | tf_op jit(solution)/shard_map/all_to_all | solution.py:151
  300.7 13.9 %all-to-all-start.7 = ((f32[8,16,256]{2,0,1:T(8,128)}), f32[8,16,256]{2,0,1:T(8,128)S(1)}, u32[]{:S(2)}, u32[]{:S(2)}) async-start(f32[8,16,256]{2,0,1:T(8,128)} %fusion.30), calls=%async_computation.7 | async-start | bytes 262144 | tf_op jit(solution)/shard_map/all_to_all | solution.py:168
  318.4 8.2 %all-to-all-done.7 = f32[8,16,256]{2,0,1:T(8,128)S(1)} async-done(((f32[8,16,256]{2,0,1:T(8,128)}), f32[8,16,256]{2,0,1:T(8,128)S(1)}, u32[]{:S(2)}, u32[]{:S(2)}) %all-to-all-start.7) | async-done | bytes 131104 | tf_op jit(solution)/shard_map/all_to_all | solution.py:168
  326.6 3.4 all-to-all-start.2
  332.7 11.5 %all-to-all-done.2 = f32[1,128,256]{2,0,1:T(1,128)S(1)} async-done(((f32[1,128,256]{2,0,1:T(1,128)}), f32[1,128,256]{2,0,1:T(1,128)S(1)}, u32[]{:S(2)}, u32[]{:S(2)}) %all-to-all-start.2) | async-done | bytes 131104 | tf_op jit(solution)/shard_map/all_to_all | solution.py:154
  344.2 6.7 %all-to-all-start.8 = ((f32[128,1,256]{2,1,0:T(1,128)}), f32[128,1,256]{2,1,0:T(1,128)S(1)}, u32[]{:S(2)}, u32[]{:S(2)}) async-start(f32[128,1,256]{2,1,0:T(1,128)} %bitcast.101), calls=%async_computation.8 | async-start | bytes 262144 | tf_op jit(solution)/shard_map/all_to_all | solution.py:171
  353.0 10.0 %all-to-all-done.8 = f32[128,1,256]{2,1,0:T(1,128)S(1)} async-done(((f32[128,1,256]{2,1,0:T(1,128)}), f32[128,1,256]{2,1,0:T(1,128)S(1)}, u32[]{:S(2)}, u32[]{:S(2)}) %all-to-all-start.8) | async-done | bytes 131104 | tf_op jit(solution)/shard_map/all_to_all | solution.py:171
  362.9 3.3 all-to-all-start.5
  366.3 4.8 %all-to-all-done.5 = f32[4,2,16,256]{3,2,1,0:T(8,128)S(1)} async-done(((f32[4,2,16,256]{3,2,1,0:T(8,128)}), f32[4,2,16,256]{3,2,1,0:T(8,128)S(1)}, u32[]{:S(2)}, u32[]{:S(2)}) %all-to-all-start.5) | async-done | bytes 131104 | tf_op jit(solution)/shard_map/all_to_all | solution.py:162
  (337 shorter events, 95.7 us)
Async XLA Ops:
  2.4 17.6 %collective-permute-start = (f32[8,3,256]{2,0,1:T(8,128)S(1)}, f32[8,3,256]{2,0,1:T(8,128)S(1)}, u32[]{:S(2)}, u32[]{:S(2)}) collective-permute-start(f32[8,3,256]{2,0,1:T(8,128)S(1)} %get-tuple-element.94), channel_id=1, source_target_pairs={{0,64},{64,128},{128,192},{192,256},{256,320},{320,384},{384,448},... | collective-permute-start | bytes 73736 | tf_op jit(solution)/shard_map/ppermute | solution.py:18
  18.7 13.3 %collective-permute-start.1 = (f32[8,3,256]{2,0,1:T(8,128)S(1)}, f32[8,3,256]{2,0,1:T(8,128)S(1)}, u32[]{:S(2)}, u32[]{:S(2)}) collective-permute-start(f32[8,3,256]{2,0,1:T(8,128)S(1)} %get-tuple-element.93), channel_id=1, source_target_pairs={{64,0},{128,64},{192,128},{256,192},{320,256},{384,320},{448,384},... | collective-permute-start | bytes 73736 | tf_op jit(solution)/shard_map/ppermute | solution.py:19
  32.0 4.8 %collective-permute-start.2 = (f32[8,22,3]{2,0,1:T(8,128)S(1)}, f32[8,22,3]{2,0,1:T(8,128)S(1)}, u32[]{:S(2)}, u32[]{:S(2)}) collective-permute-start(f32[8,22,3]{2,0,1:T(8,128)S(1)} %get-tuple-element.74), channel_id=1, source_target_pairs={{0,16},{16,32},{32,48},{1,17},{17,33},{33,49},{2,18},{18,34},{34,5... | collective-permute-start | bytes 6344 | tf_op jit(solution)/shard_map/ppermute | solution.py:18
  35.2 5.3 %collective-permute-start.3 = (f32[8,22,3]{2,0,1:T(8,128)S(1)}, f32[8,22,3]{2,0,1:T(8,128)S(1)}, u32[]{:S(2)}, u32[]{:S(2)}) collective-permute-start(f32[8,22,3]{2,0,1:T(8,128)S(1)} %get-tuple-element.75), channel_id=1, source_target_pairs={{16,0},{32,16},{48,32},{17,1},{33,17},{49,33},{18,2},{34,18},{50,3... | collective-permute-start | bytes 6344 | tf_op jit(solution)/shard_map/ppermute | solution.py:19
  40.7 11.9 %collective-permute-start.4 = (f32[3,22,262]{2,0,1:T(4,128)S(1)}, f32[3,22,262]{2,0,1:T(4,128)S(1)}, u32[]{:S(2)}, u32[]{:S(2)}) collective-permute-start(f32[3,22,262]{2,0,1:T(4,128)S(1)} %get-tuple-element.66), channel_id=1, source_target_pairs={{0,1},{1,2},{2,3},{3,4},{4,5},{5,6},{6,7},{7,8},{8,9},{9,10},{10,1... | collective-permute-start | bytes 207512 | tf_op jit(solution)/shard_map/ppermute | solution.py:18
  46.8 6.3 %collective-permute-start.5 = (f32[3,22,262]{2,0,1:T(4,128)S(1)}, f32[3,22,262]{2,0,1:T(4,128)S(1)}, u32[]{:S(2)}, u32[]{:S(2)}) collective-permute-start(f32[3,22,262]{2,0,1:T(4,128)S(1)} %get-tuple-element.67), channel_id=1, source_target_pairs={{1,0},{2,1},{3,2},{4,3},{5,4},{6,5},{7,6},{8,7},{9,8},{10,9},{11,1... | collective-permute-start | bytes 207512 | tf_op jit(solution)/shard_map/ppermute | solution.py:19
  48.7 54.4 %all-to-all-start.3 = ((f32[8,16,256]{2,1,0:T(8,128)}), f32[8,16,256]{2,1,0:T(8,128)S(1)}, u32[]{:S(2)}, u32[]{:S(2)}) async-start(f32[8,16,256]{2,1,0:T(8,128)} %param.1), calls=%async_computation.3 | async-start | bytes 262144 | tf_op jit(solution)/shard_map/all_to_all | solution.py:157
  54.9 4.4 %collective-permute-start.6 = (f32[3,8,3,256]{3,1,2,0:T(8,128)S(1)}, f32[3,8,3,256]{3,1,2,0:T(8,128)S(1)}, u32[]{:S(2)}, u32[]{:S(2)}) collective-permute-start(f32[3,8,3,256]{3,1,2,0:T(8,128)S(1)} %get-tuple-element.62), channel_id=1, source_target_pairs={{0,64},{64,128},{128,192},{192,256},{256,320},{320,384},{384,448},... | collective-permute-start | bytes 221192 | tf_op jit(solution)/shard_map/ppermute | solution.py:18
  57.9 17.6 %collective-permute-start.7 = (f32[3,8,3,256]{3,1,2,0:T(8,128)S(1)}, f32[3,8,3,256]{3,1,2,0:T(8,128)S(1)}, u32[]{:S(2)}, u32[]{:S(2)}) collective-permute-start(f32[3,8,3,256]{3,1,2,0:T(8,128)S(1)} %get-tuple-element.63), channel_id=1, source_target_pairs={{64,0},{128,64},{192,128},{256,192},{320,256},{384,320},{448,384},... | collective-permute-start | bytes 221192 | tf_op jit(solution)/shard_map/ppermute | solution.py:19
  75.7 9.3 %collective-permute-start.8 = (f32[3,8,22,3]{3,1,2,0:T(8,128)S(1)}, f32[3,8,22,3]{3,1,2,0:T(8,128)S(1)}, u32[]{:S(2)}, u32[]{:S(2)}) collective-permute-start(f32[3,8,22,3]{3,1,2,0:T(8,128)S(1)} %get-tuple-element.53), channel_id=1, source_target_pairs={{0,16},{16,32},{32,48},{1,17},{17,33},{33,49},{2,18},{18,34},{34,5... | collective-permute-start | bytes 19016 | tf_op jit(solution)/shard_map/ppermute | solution.py:18
  79.4 9.4 %collective-permute-start.9 = (f32[3,8,22,3]{3,1,2,0:T(8,128)S(1)}, f32[3,8,22,3]{3,1,2,0:T(8,128)S(1)}, u32[]{:S(2)}, u32[]{:S(2)}) collective-permute-start(f32[3,8,22,3]{3,1,2,0:T(8,128)S(1)} %get-tuple-element.54), channel_id=1, source_target_pairs={{16,0},{32,16},{48,32},{17,1},{33,17},{49,33},{18,2},{34,18},{50,3... | collective-permute-start | bytes 19016 | tf_op jit(solution)/shard_map/ppermute | solution.py:19
  90.2 29.8 %collective-permute-start.10 = (f32[3,3,22,262]{3,1,2,0:T(4,128)}, f32[3,3,22,262]{3,1,2,0:T(4,128)}, u32[]{:S(2)}, u32[]{:S(2)}) collective-permute-start(f32[3,3,22,262]{3,1,2,0:T(4,128)} %get-tuple-element.51), channel_id=1, source_target_pairs={{0,1},{1,2},{2,3},{3,4},{4,5},{5,6},{6,7},{7,8},{8,9},{9,10},{10,1... | collective-permute-start | bytes 622520 | tf_op jit(solution)/shard_map/ppermute | solution.py:18
  100.8 19.2 %collective-permute-start.11 = (f32[3,3,22,262]{3,1,2,0:T(4,128)}, f32[3,3,22,262]{3,1,2,0:T(4,128)}, u32[]{:S(2)}, u32[]{:S(2)}) collective-permute-start(f32[3,3,22,262]{3,1,2,0:T(4,128)} %get-tuple-element.52), channel_id=1, source_target_pairs={{1,0},{2,1},{3,2},{4,3},{5,4},{6,5},{7,6},{8,7},{9,8},{10,9},{11,1... | collective-permute-start | bytes 622520 | tf_op jit(solution)/shard_map/ppermute | solution.py:19
  103.1 26.5 %all-to-all-start = ((f32[8,16,256]{2,1,0:T(8,128)}), f32[8,16,256]{2,1,0:T(8,128)S(1)}, u32[]{:S(2)}, u32[]{:S(2)}) async-start(f32[8,16,256]{2,1,0:T(8,128)} %param.1), calls=%async_computation | async-start | bytes 262144 | tf_op jit(solution)/shard_map/all_to_all | solution.py:150
  129.6 8.1 %all-to-all-start.4 = ((f32[8,16,256]{2,1,0:T(8,128)}), f32[8,16,256]{2,1,0:T(8,128)S(1)}, u32[]{:S(2)}, u32[]{:S(2)}) async-start(f32[8,16,256]{2,1,0:T(8,128)} %copy.189), calls=%async_computation.4 | async-start | bytes 262144 | tf_op jit(solution)/shard_map/all_to_all | solution.py:158
  134.0 11.7 %copy-start.1 = (f32[1,128,256]{2,0,1:T(1,128)}, f32[1,128,256]{2,0,1:T(1,128)S(1)}, u32[]{:S(2)}) copy-start(f32[1,128,256]{2,0,1:T(1,128)S(1)} %all_to_all.96) | copy-start | bytes 393220
  134.0 11.7 %copy-start.3 = (f32[1,64,256]{2,0,1:T(1,128)}, f32[1,64,256]{2,0,1:T(1,128)S(1)}, u32[]{:S(2)}) copy-start(f32[1,64,256]{2,0,1:T(1,128)S(1)} %slice.1195) | copy-start | bytes 196612
  137.8 134.5 %all-to-all-start.6 = ((f32[8,16,256]{2,0,1:T(8,128)}), f32[8,16,256]{2,0,1:T(8,128)}, u32[]{:S(2)}, u32[]{:S(2)}) async-start(f32[8,16,256]{2,0,1:T(8,128)} %copy.184), calls=%async_computation.6 | async-start | bytes 262144 | tf_op jit(solution)/shard_map/all_to_all | solution.py:167
  261.8 9.4 %copy-start = (f32[2,16,128]{1,2,0:T(8,128)S(1)}, f32[2,16,128]{1,2,0:T(8,128)}, u32[]{:S(2)}) copy-start(f32[2,16,128]{1,2,0:T(8,128)} %slice.1308) | copy-start | bytes 49156
  272.2 28.5 %all-to-all-start.1 = ((f32[8,16,256]{2,1,0:T(8,128)}), f32[8,16,256]{2,1,0:T(8,128)S(1)}, u32[]{:S(2)}, u32[]{:S(2)}) async-start(f32[8,16,256]{2,1,0:T(8,128)} %copy.187), calls=%async_computation.1 | async-start | bytes 262144 | tf_op jit(solution)/shard_map/all_to_all | solution.py:151
  288.1 27.0 %copy-start.2 = (f32[1,128,256]{2,0,1:T(1,128)S(1)}, f32[1,128,256]{2,0,1:T(1,128)}, u32[]{:S(2)}) copy-start(f32[1,128,256]{2,0,1:T(1,128)} %copy-done.1) | copy-start | bytes 393220
  288.1 27.0 %slice-start = ((f32[1,64,256]{2,0,1:T(1,128)}), f32[1,63,256]{2,0,1:T(1,128)S(1)}, s32[]{:S(2)}) async-start(f32[1,64,256]{2,0,1:T(1,128)} %copy-done.3), calls=%async_computation.9 | async-start | bytes 129024 | tf_op jit(solution)/shard_map/slice | solution.py:60
  300.7 25.9 %all-to-all-start.7 = ((f32[8,16,256]{2,0,1:T(8,128)}), f32[8,16,256]{2,0,1:T(8,128)S(1)}, u32[]{:S(2)}, u32[]{:S(2)}) async-start(f32[8,16,256]{2,0,1:T(8,128)} %fusion.30), calls=%async_computation.7 | async-start | bytes 262144 | tf_op jit(solution)/shard_map/all_to_all | solution.py:168
  326.6 17.6 %all-to-all-start.2 = ((f32[1,128,256]{2,0,1:T(1,128)}), f32[1,128,256]{2,0,1:T(1,128)S(1)}, u32[]{:S(2)}, u32[]{:S(2)}) async-start(f32[1,128,256]{2,0,1:T(1,128)} %bitcast.24), calls=%async_computation.2 | async-start | bytes 262144 | tf_op jit(solution)/shard_map/all_to_all | solution.py:154
  344.2 18.8 %all-to-all-start.8 = ((f32[128,1,256]{2,1,0:T(1,128)}), f32[128,1,256]{2,1,0:T(1,128)S(1)}, u32[]{:S(2)}, u32[]{:S(2)}) async-start(f32[128,1,256]{2,1,0:T(1,128)} %bitcast.101), calls=%async_computation.8 | async-start | bytes 262144 | tf_op jit(solution)/shard_map/all_to_all | solution.py:171
  362.9 8.1 %all-to-all-start.5 = ((f32[4,2,16,256]{3,2,1,0:T(8,128)}), f32[4,2,16,256]{3,2,1,0:T(8,128)S(1)}, u32[]{:S(2)}, u32[]{:S(2)}) async-start(f32[4,2,16,256]{3,2,1,0:T(8,128)} %pad_maximum_fusion.20), calls=%async_computation.5 | async-start | bytes 262144 | tf_op jit(solution)/shard_map/all_to_all | solution.py:162
